TPU v7x, 512 devices: a whole 4x8x8 slice. The times are simulated.
512 devices in a mesh: section: 16 (over y_hi, x, core), dp: 4 (over y_lo), mp: 8 (over z).
Axes of the slice: x: 4, y: 8 (y_hi: 2, y_lo: 4; y = y_hi * 4 + y_lo), z: 8, core: 2. Of those that a mesh axis runs over, the one named last changes fastest.
Arguments:
- token_ids: int32 [16384], P(('section', 'dp')), may hold values from 0 to 127999, as said below
- table: bfloat16 [128000, 4608], P(('section', 'dp'), 'mp')
- norm_weight: float32 [4608], P('mp'), may hold values from -0.5 to 0.5
- cotangent: bfloat16 [16384, 4608], P(('section', 'dp'), 'mp')
Outputs:
- normed: bfloat16 [16384, 4608], P(('section', 'dp'), 'mp')
- weight_grad: float32 [4608], P('mp')
- table_grad: bfloat16 [128000, 4608], P(('section', 'dp'), 'mp')
Inputs may be any that keep to these rules, and one draw needn't show every extreme that they name: Owner j holds ids j * 2000 to (j + 1) * 2000 - 1. Among the 256 tokens of one device (aligned blocks of token_ids), at most 8 ids fall in any one owner's block; in every draw one owner receives exactly 8 ids from every device.
All inputs are finite; a program needn't handle non-finite values.
Results may differ from a plain program's by a relative error of at most 0.0026.
Values may be sent and summed in bfloat16 or wider, within the bound.
A program may use at most 64 MiB of HBM per device.

v0:
```python
import math

import jax
import jax.numpy as jnp
from jax import lax
from jax.sharding import PartitionSpec as P


def body(token_ids, table, norm_weight, cotangent):
    rows = table.shape[0]
    part_width = table.shape[1]
    sections = lax.axis_size("section")
    groups = lax.axis_size("dp")
    owners = sections * groups
    count = token_ids.shape[0]
    cap = 2 * count // owners
    width = part_width * lax.axis_size("mp")
    owner_of = token_ids // rows
    within_ids = token_ids - owner_of * rows
    member = (owner_of[:, None] == jnp.arange(owners, dtype=jnp.int32)[None, :]).astype(jnp.int32)
    earlier = jnp.cumsum(member, axis=0) - member
    rank_in = jnp.sum(earlier * member, axis=1)
    slot_of = owner_of * cap + rank_in
    requests = (
        jnp.full((owners * cap,), -1, jnp.int32).at[slot_of].set(within_ids).reshape(owners, cap)
    )
    asked = lax.all_to_all(requests, ("section", "dp"), split_axis=0, concat_axis=0, tiled=True)
    valid = asked >= 0
    fetched = jnp.take(table, jnp.clip(asked, 0, rows - 1), axis=0)
    answer = lax.all_to_all(
        jnp.where(valid[..., None], fetched, jnp.zeros_like(fetched)),
        ("section", "dp"),
        split_axis=0,
        concat_axis=0,
        tiled=True,
    )
    embedded = answer.reshape(owners * cap, part_width)[slot_of]
    scale = math.sqrt(width)
    scaled = embedded.astype(jnp.float32) * scale
    squares = lax.psum(jnp.sum(scaled * scaled, axis=1), "mp")
    inv_rms = lax.rsqrt(squares / width + 1e-06)
    unit = scaled * inv_rms[:, None]
    multiplier = 1.0 + norm_weight
    normed = (unit * multiplier[None, :]).astype(jnp.bfloat16)
    incoming = cotangent.astype(jnp.float32)
    weight_grad = lax.psum(jnp.sum(incoming * unit, axis=0), ("section", "dp"))
    grad_hat = incoming * multiplier[None, :]
    inner = lax.psum(jnp.sum(grad_hat * unit, axis=1), "mp") / width
    grad_embed = (scale * inv_rms[:, None] * (grad_hat - unit * inner[:, None])).astype(
        jnp.bfloat16
    )
    grad_slots = jnp.zeros((owners * cap, part_width), jnp.bfloat16).at[slot_of].set(grad_embed)
    arrived = lax.all_to_all(
        grad_slots.reshape(owners, cap, part_width),
        ("section", "dp"),
        split_axis=0,
        concat_axis=0,
        tiled=True,
    )
    flat_ids = asked.reshape(owners * cap)
    keep = flat_ids >= 0
    values = jnp.where(
        keep[:, None], arrived.reshape(owners * cap, part_width).astype(jnp.float32), 0.0
    )
    table_grad = (
        jnp.zeros((rows, part_width), jnp.float32).at[jnp.clip(flat_ids, 0, rows - 1)].add(values)
    )
    return (normed, weight_grad, table_grad.astype(jnp.bfloat16))


def solution(mesh):
    placed = (P(("section", "dp")), P(("section", "dp"), "mp"), P("mp"), P(("section", "dp"), "mp"))
    return jax.shard_map(
        body,
        mesh=mesh,
        in_specs=placed,
        out_specs=(P(("section", "dp"), "mp"), P("mp"), P(("section", "dp"), "mp")),
        check_vma=False,
    )
```

profile of v0, /device:TPU:32, one launch (start us, length us, event | category | flops | bytes accessed | tf_op | source)
XLA Modules:
  0.0 249.7 jit_solution(8181027631193016140)
XLA Ops:
  0.6 0.7 multiply_subtract_fusion
  1.3 0.6 reduce-window.6
  1.9 0.2 slice_reduce_fusion
  2.3 1.4 scatter_custom_fusion
  3.7 0.7 all_to_all.12
  4.4 10.3 %all-to-all-start = ((s32[64,1,8]{2,1,0:T(1,128)}), s32[64,1,8]{2,1,0:T(1,128)S(1)}, u32[]{:S(2)}, u32[]{:S(2)}) async-start(s32[64,1,8]{2,1,0:T(1,128)} %bitcast.2), calls=%async_computation | async-start | bytes 65536 | tf_op jit(solution)/shard_map/all_to_all | solution.py:27
  14.7 3.6 %copy.28 = bf16[2000,576]{1,0:T(8,128)(2,1)S(1)} copy(bf16[2000,576]{0,1:T(8,128)(2,1)} %param.5) | data formatting | bytes 4608000 | tf_op args[1]
  18.3 0.9 all-to-all-done
  19.7 2.0 gather_fusion
  21.8 1.1 fusion.14
  22.8 9.8 %all-to-all-start.1 = ((bf16[64,8,576]{2,1,0:T(8,128)(2,1)}), bf16[64,8,576]{2,1,0:T(8,128)(2,1)S(1)}, u32[]{:S(2)}, u32[]{:S(2)}) async-start(bf16[64,8,576]{2,1,0:T(8,128)(2,1)} %fusion.14), calls=%async_computation.1 | async-start | bytes 1310720 | tf_op jit(solution)/shard_map/all_to_all | solution.py:30
  32.6 0.2 copy.29
  32.9 16.8 %all-to-all-done.1 = bf16[64,8,576]{2,1,0:T(8,128)(2,1)S(1)} async-done(((bf16[64,8,576]{2,1,0:T(8,128)(2,1)}), bf16[64,8,576]{2,1,0:T(8,128)(2,1)S(1)}, u32[]{:S(2)}, u32[]{:S(2)}) %all-to-all-start.1) | async-done | bytes 589856 | tf_op jit(solution)/shard_map/all_to_all | solution.py:30
  49.7 1.2 gather_fusion.1
  51.0 23.2 %psum.21 = f32[256]{0:T(256)S(1)} all-reduce(f32[256]{0:T(256)S(1)} %fusion.11), channel_id=1, replica_groups=mesh['section'=16,'dp'=4,'mp'=8] {'mp'}, use_global_device_ids=true, to_apply=%region_5.6 | all-reduce | flops 256 | bytes 2048 | tf_op jit(solution)/shard_map/psum | solution.py:40
  74.2 0.4 fusion.9
  74.7 14.2 %psum.23 = f32[256]{0:T(256)S(1)} all-reduce(f32[256]{0:T(256)S(1)} %get-tuple-element.15), channel_id=1, replica_groups=mesh['section'=16,'dp'=4,'mp'=8] {'mp'}, use_global_device_ids=true, to_apply=%region_9.10 | all-reduce | flops 256 | bytes 2048 | tf_op jit(solution)/shard_map/psum | solution.py:48
  88.8 2.7 %scatter_custom_fusion.1 = bf16[512,576]{1,0:T(8,128)(2,1)} fusion(s32[256]{0:T(256)S(1)} %compare_select_fusion.3, bf16[256,576]{1,0:T(8,128)(2,1)S(1)} %copy.29, bf16[256,576]{1,0:T(8,128)(2,1)S(1)} %gather_fusion.1, f32[256]{0:T(256)S(1)} %broadcast_multiply_fusion, bf16[]{:T(256)} %constant.26.clone.1, f32[576]{0:T(1024)S(1)} %broadcast_add_fusion, ...), kind=kCustom, calls=%fused_computation.28 | custom fusion | flops 1179648 | bytes 1251330 | tf_op jit(solution)/shard_map/scatter | solution.py:52
  91.5 9.2 %all-to-all-start.2 = ((bf16[64,8,576]{2,1,0:T(8,128)(2,1)}), bf16[64,8,576]{2,1,0:T(8,128)(2,1)S(1)}, u32[]{:S(2)}, u32[]{:S(2)}) async-start(bf16[64,8,576]{2,1,0:T(8,128)(2,1)} %bitcast.9), calls=%async_computation.2 | async-start | bytes 1310720 | tf_op jit(solution)/shard_map/all_to_all | solution.py:53
  101.1 0.9 copy.32
  102.0 135.4 %psum.22 = f32[576]{0:T(1024)} all-reduce(f32[576]{0:T(1024)S(1)} %get-tuple-element.16), channel_id=1, replica_groups=mesh['section'=16,'dp'=4,'mp'=8] {'section','dp'}, use_global_device_ids=true, to_apply=%region_7.8 | all-reduce | flops 576 | bytes 4608 | tf_op jit(solution)/shard_map/psum | solution.py:46
  237.4 6.6 %scatter_custom_fusion.2 = f32[2000,576]{1,0:T(8,128)} fusion(s32[512]{0:T(512)S(1)} %bitcast.52, f32[]{:T(128)} %constant.28.clone.1, bf16[64,8,576]{2,1,0:T(8,128)(2,1)S(1)} %all-to-all-done.2, pred[512]{0:T(512)(128)(4,1)S(1)} %ge.40), kind=kCustom, calls=%fused_computation.5 | custom fusion | flops 884736 | bytes 5264896 | tf_op jit(solution)/shard_map/scatter-add | solution.py:66
  244.0 2.7 %convert_element_type.36 = bf16[2000,576]{1,0:T(8,128)(2,1)S(1)} convert(f32[2000,576]{1,0:T(8,128)} %scatter_custom_fusion.2) | non-fusion elementwise | flops 1152000 | bytes 6912000 | tf_op jit(solution)/shard_map/convert_element_type | solution.py:68
  246.7 3.0 %copy.33 = bf16[2000,576]{0,1:T(8,128)(2,1)} copy(bf16[2000,576]{1,0:T(8,128)(2,1)S(1)} %convert_element_type.36) | data formatting | bytes 4608000
  (31 shorter events, 1.3 us)
Async XLA Ops:
  4.4 14.8 %all-to-all-start = ((s32[64,1,8]{2,1,0:T(1,128)}), s32[64,1,8]{2,1,0:T(1,128)S(1)}, u32[]{:S(2)}, u32[]{:S(2)}) async-start(s32[64,1,8]{2,1,0:T(1,128)} %bitcast.2), calls=%async_computation | async-start | bytes 65536 | tf_op jit(solution)/shard_map/all_to_all | solution.py:27
  21.7 10.9 %copy-start = (bf16[256,576]{0,1:T(8,128)(2,1)S(1)}, bf16[256,576]{0,1:T(8,128)(2,1)}, u32[]{:S(2)}) copy-start(bf16[256,576]{0,1:T(8,128)(2,1)} %param.7) | copy-start | bytes 884740
  21.7 11.1 %copy-start.1 = (f32[576]{0:T(1024)S(1)}, f32[576]{0:T(1024)}, u32[]{:S(2)}) copy-start(f32[576]{0:T(1024)} %param.6) | copy-start | bytes 6916
  22.8 26.9 %all-to-all-start.1 = ((bf16[64,8,576]{2,1,0:T(8,128)(2,1)}), bf16[64,8,576]{2,1,0:T(8,128)(2,1)S(1)}, u32[]{:S(2)}, u32[]{:S(2)}) async-start(bf16[64,8,576]{2,1,0:T(8,128)(2,1)} %fusion.14), calls=%async_computation.1 | async-start | bytes 1310720 | tf_op jit(solution)/shard_map/all_to_all | solution.py:30
  91.5 145.9 %all-to-all-start.2 = ((bf16[64,8,576]{2,1,0:T(8,128)(2,1)}), bf16[64,8,576]{2,1,0:T(8,128)(2,1)S(1)}, u32[]{:S(2)}, u32[]{:S(2)}) async-start(bf16[64,8,576]{2,1,0:T(8,128)(2,1)} %bitcast.9), calls=%async_computation.2 | async-start | bytes 1310720 | tf_op jit(solution)/shard_map/all_to_all | solution.py:53
where the time goes:
time: 250 us
  blocking collectives  173 us (69%)
  starting transfers between devices  29.3 us (12%)
  waiting for transfers between devices  17.7 us (7%)
  other arithmetic  15.2 us (6%)
  local copies, waits for them, and re-layouts  14 us (6%)
    psum x1, blocking collectives, body(): weight_grad = lax.psum(jnp.sum(incoming * unit, axis=0), ('section', 'dp'))  135 us
    psum x1, blocking collectives, body(): squares = lax.psum(jnp.sum(scaled * scaled, axis=1), 'mp')  23.2 us
    all_to_all x1, waiting for transfers between devices, body(): lax.all_to_all(jnp.where(valid[..., None], fetched, jnp.zeros_like(fetche...  16.8 us
    psum x1, blocking collectives, body(): inner = lax.psum(jnp.sum(grad_hat * unit, axis=1), 'mp') / width  14.2 us
    all_to_all x1, starting transfers between devices, body(): lax.all_to_all(requests, ('section', 'dp'), split_axis=0, concat_axis=0,...  10.3 us
    all_to_all x1, starting transfers between devices, body(): lax.all_to_all(jnp.where(valid[..., None], fetched, jnp.zeros_like(fetche...  9.78 us
    all_to_all x1, starting transfers between devices, body(): lax.all_to_all(grad_slots.reshape(owners, cap, part_width), ('section', '...  9.22 us
    unnamed x8, local copies, waits for them, and re-layouts  7.65 us
  transfers between devices with their start and end apart: 3, of which 2 were waited for; matrix products, arithmetic and copies ran while one was open for 2% of the time, Pallas kernels for 0%

commit v1 on v0

v1 whole, which is shorter than its diff:
```python
import functools
import math

import jax
import jax.numpy as jnp
from jax import lax
from jax.experimental import pallas as pl
from jax.experimental.pallas import tpu as pltpu
from jax.sharding import PartitionSpec as P

MESH = pl.DeviceIdType.MESH
F32 = jnp.float32
BF16 = jnp.bfloat16
EPS = 1e-06
NT = (((1,), (1,)), ((), ()))
TN = (((0,), (0,)), ((), ()))

CHUNK = 128


def kernel(
    dims,
    ids_ref,
    weight_ref,
    cot_ref,
    table_hbm,
    normed_ref,
    wg_ref,
    grad_hbm,
    table_ref,
    ext_ref,
    place_ref,
    send_ref,
    recv_ref,
    hot_ref,
    rows_ref,
    part_ref,
    zbuf_ref,
    back_ref,
    done_ref,
    g_ref,
    grad_ref,
    wgp_ref,
    wg1_ref,
    wgs_ref,
    wg2_ref,
    sems,
):
    groups, ring, cap, cores = dims
    owners = lax.axis_size("section") * groups
    heights = owners // cores
    width, count = cot_ref.shape
    vrows = table_ref.shape[1]
    slots = owners * cap
    scale = math.sqrt(width * ring)
    chunks = slots // CHUNK
    per = CHUNK // cap

    sec = lax.axis_index("section")
    grp = lax.axis_index("dp")
    col = lax.axis_index("mp")
    me = sec * groups + grp
    inner_id = lax.rem(sec, cores)
    height = lax.div(sec, cores) * groups + grp

    def plane(step):
        p = lax.rem(me + step, owners)
        return p, (lax.div(p, groups), lax.rem(p, groups), col)

    def along(step):
        return (sec, grp, lax.rem(col + step, ring))

    def beside(step):
        return (sec - inner_id + lax.rem(inner_id + step, cores), grp, col)

    def above(step):
        h = lax.rem(height + step, heights)
        return (lax.div(h, groups) * cores + inner_id, lax.rem(h, groups), col)

    barrier = pltpu.get_barrier_semaphore()

    @pl.loop(1, owners)
    def _(k):
        pl.semaphore_signal(barrier, inc=1, device_id=plane(k)[1], device_id_type=MESH)

    @pl.loop(1, ring)
    def _(k):
        pl.semaphore_signal(barrier, inc=1, device_id=along(k), device_id_type=MESH)

    table_copy = pltpu.make_async_copy(table_hbm, table_ref, sems.at[0])
    table_copy.start()

    ids = jnp.broadcast_to(ids_ref[...], (owners, count))
    local = ids - vrows * lax.broadcasted_iota(jnp.int32, (owners, count), 0)
    member = (local >= 0) & (local < vrows)
    before = lax.broadcasted_iota(jnp.int32, (count, count), 0) < lax.broadcasted_iota(
        jnp.int32, (count, count), 1
    )
    rank = jnp.dot(
        jnp.where(member, 1.0, 0.0).astype(BF16),
        jnp.where(before, 1.0, 0.0).astype(BF16),
        preferred_element_type=F32,
    )
    rank = jnp.where(member, rank, -1.0)
    slot_of = lax.broadcasted_iota(jnp.int32, (owners, cap, count), 1).astype(F32)
    place = jnp.where(rank[:, None, :] == slot_of, 1.0, 0.0).reshape(slots, count)
    place_ref[...] = place.astype(BF16)
    within = jnp.sum(jnp.where(member, local, 0), axis=0, keepdims=True)
    extra = ext_ref.shape[0] - width
    within = jnp.broadcast_to(within, (extra, count))
    line = lax.broadcasted_iota(jnp.int32, (extra, count), 0)
    code = jnp.where(line == 0, (within >> 6) + 1, jnp.where(line == 1, within & 63, 0))
    ext_ref[:width, :] = cot_ref[...]
    ext_ref[width:, :] = code.astype(F32).astype(BF16)
    for q in range(chunks):
        packed = lax.dot_general(
            place_ref[q * CHUNK : (q + 1) * CHUNK, :], ext_ref[...], NT, preferred_element_type=F32
        )
        send_ref[q * per : (q + 1) * per] = packed.reshape(per, cap, -1).astype(BF16)

    pl.semaphore_wait(barrier, owners - 1 + ring - 1)

    def exchange(src, dst, send_sem, recv_sem):
        @pl.loop(1, owners)
        def _(k):
            p, device = plane(k)
            pltpu.make_async_remote_copy(
                src_ref=src.at[p],
                dst_ref=dst.at[me],
                send_sem=send_sem,
                recv_sem=recv_sem,
                device_id=device,
                device_id_type=MESH,
            ).start()

    def wait_blocks(ref, number, sem):
        part = ref.at[pl.ds(0, number)]
        pltpu.make_async_copy(part, part, sem).wait()

    exchange(send_ref, recv_ref, sems.at[1], sems.at[2])
    recv_ref[me] = send_ref[me]
    table_copy.wait()
    multiplier = 1.0 + weight_ref[...]
    wait_blocks(recv_ref, owners - 1, sems.at[2])

    def received(q):
        block = recv_ref[q * per : (q + 1) * per].astype(F32)
        return block.reshape(CHUNK, block.shape[2])

    lane = lax.broadcasted_iota(jnp.int32, (CHUNK, 128), 1)
    for q in range(chunks):
        here = slice(q * CHUNK, (q + 1) * CHUNK)
        block = received(q)
        wanted = (block[:, width : width + 1] - 1.0) * 64.0 + block[:, width + 1 : width + 2]
        entry = lax.broadcasted_iota(jnp.int32, (CHUNK, vrows), 1).astype(F32)
        hot_ref[here, :] = jnp.where(wanted == entry, 1.0, 0.0).astype(BF16)
        rows = lax.dot_general(
            hot_ref[here, :], table_ref[...], NT, preferred_element_type=F32
        )
        rows_ref[here, :] = rows
        squares = jnp.sum(rows * rows, axis=1, keepdims=True)
        near = lax.rsqrt(squares + EPS)
        product = jnp.sum(block[:, :width] * multiplier * (rows * near), axis=1, keepdims=True)
        both = jnp.where(lane == 0, squares, jnp.where(lane == 1, product, 0.0)).T
        part_ref[q : q + 1, :] = both[0:1, :]
        part_ref[chunks + q : chunks + q + 1, :] = both[1:2, :]

    @pl.loop(1, ring)
    def _(k):
        pltpu.make_async_remote_copy(
            src_ref=part_ref,
            dst_ref=zbuf_ref.at[col],
            send_sem=sems.at[3],
            recv_sem=sems.at[4],
            device_id=along(k),
            device_id_type=MESH,
        ).start()

    zbuf_ref[col] = part_ref[...]
    wait_blocks(zbuf_ref, ring - 1, sems.at[4])

    squares = jnp.zeros((chunks, 128), F32)
    product = jnp.zeros((chunks, 128), F32)
    for z in range(ring):
        theirs = zbuf_ref[z, :chunks, :]
        squares += theirs
        product += zbuf_ref[z, chunks:, :] / lax.rsqrt(theirs + EPS)
    inverse = lax.rsqrt(squares + EPS)
    product = product * inverse * (scale / (width * ring))
    columns = jnp.concatenate(
        [inverse, product, jnp.zeros((128 - 2 * chunks, 128), F32)], axis=0
    ).T
    total = jnp.zeros((1, width), F32)
    for q in range(chunks):
        here = slice(q * CHUNK, (q + 1) * CHUNK)
        inv_rms = columns[:, q : q + 1]
        inner = columns[:, chunks + q : chunks + q + 1]
        incoming = received(q)[:, :width]
        unit = rows_ref[here, :] * scale * inv_rms
        normed = unit * multiplier
        back_ref[q * per : (q + 1) * per, :, :width] = normed.reshape(per, cap, width).astype(BF16)
        total += jnp.sum(incoming * unit, axis=0, keepdims=True)
        grad_hat = incoming * multiplier
        g_ref[here, :] = (scale * inv_rms * (grad_hat - unit * inner)).astype(BF16)
    back_ref[:, :, width:] = jnp.zeros((owners, cap, extra), BF16)

    wgp_ref[:, :width] = total
    wgp_ref[:, width:] = jnp.zeros((1, extra), F32)

    def gather_sum(src, dst, mine, number, device_of, send_sem, recv_sem):
        @pl.loop(1, number)
        def _(k):
            pltpu.make_async_remote_copy(
                src_ref=src,
                dst_ref=dst.at[mine],
                send_sem=send_sem,
                recv_sem=recv_sem,
                device_id=device_of(k),
                device_id_type=MESH,
            ).start()

        dst[mine] = src[...]

    gather_sum(wgp_ref, wg1_ref, inner_id, cores, beside, sems.at[5], sems.at[6])
    exchange(back_ref, done_ref, sems.at[7], sems.at[8])
    done_ref[me] = back_ref[me]
    wait_blocks(wg1_ref, cores - 1, sems.at[6])
    wgs_ref[...] = jnp.sum(wg1_ref[...], axis=0)
    gather_sum(wgs_ref, wg2_ref, height, heights, above, sems.at[9], sems.at[10])

    grad_ref[...] = lax.dot_general(
        g_ref[...], hot_ref[...], TN, preferred_element_type=F32
    ).astype(BF16)
    grad_copy = pltpu.make_async_copy(grad_ref, grad_hbm, sems.at[0])
    grad_copy.start()

    wait_blocks(wg2_ref, heights - 1, sems.at[10])
    wg_ref[...] = jnp.sum(wg2_ref[...], axis=0)[:, :width]
    wait_blocks(done_ref, owners - 1, sems.at[8])
    arrived = done_ref[...].astype(F32).reshape(slots, done_ref.shape[2])[:, :width].astype(BF16)
    normed_ref[...] = lax.dot_general(
        arrived, place_ref[...], TN, preferred_element_type=F32
    ).astype(BF16)

    wait_blocks(send_ref, owners - 1, sems.at[1])
    wait_blocks(zbuf_ref, ring - 1, sems.at[3])
    wait_blocks(wg1_ref, cores - 1, sems.at[5])
    wait_blocks(back_ref, owners - 1, sems.at[7])
    wait_blocks(wg2_ref, heights - 1, sems.at[9])
    grad_copy.wait()


def body(mesh, token_ids, table, norm_weight, cotangent):
    groups, ring = mesh.shape["dp"], mesh.shape["mp"]
    owners = mesh.shape["section"] * groups
    vrows, width = table.shape
    count = token_ids.shape[0]
    cap = 2 * count // owners
    cores = 8
    heights = owners // cores
    slots = owners * cap
    wide = -(-(width + 2) // 128) * 128
    vmem = pl.BlockSpec(memory_space=pltpu.VMEM)
    hbm = pl.BlockSpec(memory_space=pl.ANY)
    normed, weight_grad, table_grad = pl.pallas_call(
        functools.partial(kernel, (groups, ring, cap, cores)),
        out_shape=(
            jax.ShapeDtypeStruct((width, count), BF16),
            jax.ShapeDtypeStruct((1, width), F32),
            jax.ShapeDtypeStruct((width, vrows), BF16),
        ),
        in_specs=[vmem, vmem, vmem, hbm],
        out_specs=(vmem, vmem, hbm),
        scratch_shapes=[
            pltpu.VMEM((width, vrows), BF16),
            pltpu.VMEM((wide, count), BF16),
            pltpu.VMEM((slots, count), BF16),
            pltpu.VMEM((owners, cap, wide), BF16),
            pltpu.VMEM((owners, cap, wide), BF16),
            pltpu.VMEM((slots, vrows), BF16),
            pltpu.VMEM((slots, width), F32),
            pltpu.VMEM((2 * slots // CHUNK, 128), F32),
            pltpu.VMEM((ring, 2 * slots // CHUNK, 128), F32),
            pltpu.VMEM((owners, cap, wide), BF16),
            pltpu.VMEM((owners, cap, wide), BF16),
            pltpu.VMEM((slots, width), BF16),
            pltpu.VMEM((width, vrows), BF16),
            pltpu.VMEM((1, wide), F32),
            pltpu.VMEM((cores, 1, wide), F32),
            pltpu.VMEM((1, wide), F32),
            pltpu.VMEM((heights, 1, wide), F32),
            pltpu.SemaphoreType.DMA((11,)),
        ],
        compiler_params=pltpu.CompilerParams(
            collective_id=0, has_side_effects=True, vmem_limit_bytes=40 * 1024 * 1024
        ),
    )(token_ids.reshape(1, count), norm_weight.reshape(1, width), cotangent.T, table.T)
    return normed.T, weight_grad.reshape(width), table_grad.T


def solution(mesh):
    placed = (P(("section", "dp")), P(("section", "dp"), "mp"), P("mp"), P(("section", "dp"), "mp"))
    return jax.shard_map(
        functools.partial(body, mesh),
        mesh=mesh,
        in_specs=placed,
        out_specs=(P(("section", "dp"), "mp"), P("mp"), P(("section", "dp"), "mp")),
        check_vma=False,
    )
```

time: 250 us -> 67.2 us (0.27)
  the two profiles are of different devices: /device:TPU:32 before, /device:TPU:6 now
where the time goes in v1:
time: 67.2 us; the launch traced here: 66.8 us
  Pallas kernels  59.4 us (88%)
  local copies, waits for them, and re-layouts  6.11 us (9%)
    pallas_call x1, Pallas kernels, body(): pl.pallas_call(functools.partial(kernel, (groups, ring, cap, cores)), out...  59.4 us
    unnamed x8, local copies, waits for them, and re-layouts  5.42 us

profile of v1, /device:TPU:6, one launch (start us, length us, event | category | flops | bytes accessed | tf_op | source)
XLA Modules:
  0.0 66.8 jit_solution(7388644146159032425)
XLA Ops:
  0.6 0.7 %reshape.16.weight_ref = f32[1,576]{1,0:T(1,128)S(1)} reshape(f32[576]{0:T(1024)} %param.6) | data formatting | bytes 4608 | tf_op jit(solution)/shard_map/reshape | solution.py:297
  1.3 0.0 copy-start
  1.3 1.7 %copy-done = bf16[2000,576]{0,1:T(8,128)(2,1)S(1)} copy-done((bf16[2000,576]{0,1:T(8,128)(2,1)S(1)}, bf16[2000,576]{0,1:T(8,128)(2,1)}, u32[]{:S(2)}) %copy-start) | copy-done | bytes 2304024
  3.0 0.0 copy-start.1
  3.0 1.0 %copy-done.1 = bf16[256,576]{0,1:T(8,128)(2,1)S(1)} copy-done((bf16[256,576]{0,1:T(8,128)(2,1)S(1)}, bf16[256,576]{0,1:T(8,128)(2,1)}, u32[]{:S(2)}) %copy-start.1) | copy-done | bytes 294936
  3.9 0.0 copy-start.2
  4.0 0.7 %copy-done.2 = s32[256]{0:T(256)S(1)} copy-done((s32[256]{0:T(256)S(1)}, s32[256]{0:T(256)}, u32[]{:S(2)}) %copy-start.2) | copy-done | bytes 1048
  4.6 59.4 %shard_map.67 = (bf16[576,256]{1,0:T(8,128)(2,1)S(1)}, f32[1,576]{1,0:T(1,128)S(1)}, bf16[576,2000]{1,0:T(8,128)(2,1)S(1)}) custom-call(s32[1,256]{1,0:T(1,128)S(1)} %bitcast.9, f32[1,576]{1,0:T(1,128)S(1)} %reshape.16.weight_ref, bf16[576,256]{1,0:T(8,128)(2,1)S(1)} %bitcast.7, bf16[576,2000]{1,0:T(8,128)(2,1)S(1)} %bitcast.5), custom_call_target="tpu_custom_call" | custom-call | tf_op jit(solution)/shard_map/pallas_call | solution.py:265
  64.1 0.6 reduce
  64.7 0.7 %copy.9 = bf16[256,576]{0,1:T(8,128)(2,1)} copy(bf16[256,576]{0,1:T(8,128)(2,1)S(1)} %bitcast.8) | data formatting | bytes 589824
  65.4 1.4 %copy.10 = bf16[2000,576]{0,1:T(8,128)(2,1)} copy(bf16[2000,576]{0,1:T(8,128)(2,1)S(1)} %bitcast.6) | data formatting | bytes 4608000
Async XLA Ops:
  1.3 1.7 %copy-start = (bf16[2000,576]{0,1:T(8,128)(2,1)S(1)}, bf16[2000,576]{0,1:T(8,128)(2,1)}, u32[]{:S(2)}) copy-start(bf16[2000,576]{0,1:T(8,128)(2,1)} %param.5) | copy-start | bytes 6912004
  3.0 1.0 %copy-start.1 = (bf16[256,576]{0,1:T(8,128)(2,1)S(1)}, bf16[256,576]{0,1:T(8,128)(2,1)}, u32[]{:S(2)}) copy-start(bf16[256,576]{0,1:T(8,128)(2,1)} %param.7) | copy-start | bytes 884740
  3.9 0.7 %copy-start.2 = (s32[256]{0:T(256)S(1)}, s32[256]{0:T(256)}, u32[]{:S(2)}) copy-start(s32[256]{0:T(256)} %param.4) | copy-start | bytes 3076

commit v2 on v1

v2 whole, which is shorter than its diff:
```python
import functools
import math

import jax
import jax.numpy as jnp
from jax import lax
from jax.experimental import pallas as pl
from jax.experimental.pallas import tpu as pltpu
from jax.sharding import PartitionSpec as P

MESH = pl.DeviceIdType.MESH
F32 = jnp.float32
BF16 = jnp.bfloat16
EPS = 1e-06
NT = (((1,), (1,)), ((), ()))
TN = (((0,), (0,)), ((), ()))

CHUNK = 128


def kernel(
    dims,
    ids_hbm,
    weight_hbm,
    cot_hbm,
    table_hbm,
    normed_ref,
    wg_ref,
    grad_ref,
    ids_ref,
    weight_ref,
    table_ref,
    cot_ref,
    place_ref,
    ask_ref,
    asked_ref,
    send_ref,
    recv_ref,
    hot_ref,
    unit_ref,
    part_ref,
    square_ref,
    inner_ref,
    back_ref,
    done_ref,
    g_ref,
    wgp_ref,
    wg1_ref,
    wgs_ref,
    wg2_ref,
    local_sems,
    send_sems,
    recv_sems,
):
    groups, ring, cap, cores = dims
    owners = lax.axis_size("section") * groups
    heights = owners // cores
    width, count = cot_ref.shape
    vrows = table_ref.shape[1]
    slots = owners * cap
    wide = send_ref.shape[2]
    scale = math.sqrt(width * ring)
    chunks = slots // CHUNK
    per = CHUNK // cap

    sec = lax.axis_index("section")
    grp = lax.axis_index("dp")
    col = lax.axis_index("mp")
    me = sec * groups + grp
    inner_id = lax.rem(sec, cores)
    height = lax.div(sec, cores) * groups + grp

    def plane(step):
        p = lax.rem(me + step, owners)
        return p, (lax.div(p, groups), lax.rem(p, groups), col)

    def along(step):
        return (sec, grp, lax.rem(col + step, ring))

    def beside(step):
        return (sec - inner_id + lax.rem(inner_id + step, cores), grp, col)

    def above(step):
        h = lax.rem(height + step, heights)
        return (lax.div(h, groups) * cores + inner_id, lax.rem(h, groups), col)

    barrier = pltpu.get_barrier_semaphore()

    @pl.loop(1, owners)
    def _(k):
        pl.semaphore_signal(barrier, inc=1, device_id=plane(k)[1], device_id_type=MESH)

    @pl.loop(1, ring)
    def _(k):
        pl.semaphore_signal(barrier, inc=1, device_id=along(k), device_id_type=MESH)

    fetches = [
        pltpu.make_async_copy(src, dst, local_sems.at[n])
        for n, (src, dst) in enumerate(
            (
                (ids_hbm, ids_ref),
                (cot_hbm, cot_ref),
                (weight_hbm, weight_ref),
                (table_hbm, table_ref),
            )
        )
    ]
    for fetch in fetches:
        fetch.start()

    before = lax.broadcasted_iota(jnp.int32, (count, count), 0) < lax.broadcasted_iota(
        jnp.int32, (count, count), 1
    )
    before = jnp.where(before, 1.0, 0.0).astype(BF16)
    fetches[0].wait()
    ids = jnp.broadcast_to(ids_ref[...], (owners, count))
    local = ids - vrows * lax.broadcasted_iota(jnp.int32, (owners, count), 0)
    member = (local >= 0) & (local < vrows)
    rank = jnp.dot(
        jnp.where(member, 1.0, 0.0).astype(BF16), before, preferred_element_type=F32
    )
    rank = jnp.where(member, rank, -1.0)
    lane = lax.broadcasted_iota(jnp.int32, (owners, 128), 1)
    wanted = jnp.full((owners, 128), -1, jnp.int32)
    for s in range(cap):
        one = jnp.sum(jnp.where(rank == s, local + 1, 0), axis=1, keepdims=True) - 1
        wanted = jnp.where(lane == s, one, wanted)
    ask_ref[...] = wanted[:, None, :]
    slot_of = lax.broadcasted_iota(jnp.int32, (owners, cap, count), 1).astype(F32)
    place = jnp.where(rank[:, None, :] == slot_of, 1.0, 0.0).reshape(slots, count)
    place_ref[...] = place.astype(BF16)

    def send_to(src, dst, n, device):
        pltpu.make_async_remote_copy(
            src_ref=src,
            dst_ref=dst,
            send_sem=send_sems.at[n],
            recv_sem=recv_sems.at[n],
            device_id=device,
            device_id_type=MESH,
        ).start()

    def exchange(src, dst, n):
        @pl.loop(1, owners)
        def _(k):
            p, device = plane(k)
            send_to(src.at[p], dst.at[me], n, device)

    def share(src, dst, n, mine, number, device_of):
        @pl.loop(1, number)
        def _(k):
            send_to(src, dst.at[mine], n, device_of(k))

        dst[mine] = src[...]

    def wait_blocks(ref, number, sem):
        part = ref.at[pl.ds(0, number)]
        pltpu.make_async_copy(part, part, sem).wait()

    pl.semaphore_wait(barrier, owners - 1 + ring - 1)
    exchange(ask_ref, asked_ref, 0)
    asked_ref[me] = ask_ref[me]

    fetches[1].wait()
    for q in range(chunks):
        packed = lax.dot_general(
            place_ref[q * CHUNK : (q + 1) * CHUNK, :], cot_ref[...], NT, preferred_element_type=F32
        )
        block = slice(q * per, (q + 1) * per)
        send_ref[block, :, :width] = packed.reshape(per, cap, width).astype(BF16)
    send_ref[:, :, width:] = jnp.zeros((owners, cap, wide - width), BF16)
    back_ref[:, :, width:] = jnp.zeros((owners, cap, wide - width), BF16)
    exchange(send_ref, recv_ref, 1)
    recv_ref[me] = send_ref[me]

    fetches[2].wait()
    multiplier = 1.0 + weight_ref[...].reshape(1, width)
    fetches[3].wait()
    wait_blocks(asked_ref, owners - 1, recv_sems.at[0])

    lane = lax.broadcasted_iota(jnp.int32, (CHUNK, 128), 1)
    own_lane = lane == lax.rem(lax.broadcasted_iota(jnp.int32, (CHUNK, 128), 0), cap)
    entry = lax.broadcasted_iota(jnp.int32, (CHUNK, vrows), 1)

    def as_rows(columns):
        out = jnp.zeros((CHUNK, 128), F32)
        for q, column in enumerate(columns):
            out = jnp.where(lane == q, column, out)
        return out.T[:chunks, :]

    def as_columns(rows):
        filler = jnp.zeros((128 - chunks, 128), F32)
        return jnp.concatenate([rows, filler], axis=0).T

    sums = []
    for q in range(chunks):
        here = slice(q * CHUNK, (q + 1) * CHUNK)
        theirs = asked_ref[q * per : (q + 1) * per]
        theirs = jnp.broadcast_to(theirs, (per, cap, 128)).reshape(CHUNK, 128)
        number = jnp.sum(jnp.where(own_lane, theirs, 0), axis=1, keepdims=True)
        hot_ref[here, :] = jnp.where(number == entry, 1.0, 0.0).astype(BF16)
        rows = lax.dot_general(hot_ref[here, :], table_ref[...], NT, preferred_element_type=F32)
        unit_ref[here, :] = rows
        sums.append(jnp.sum(rows * rows, axis=1, keepdims=True))
    part_ref[0] = as_rows(sums)
    share(part_ref.at[0], square_ref, 2, col, ring, along)
    wait_blocks(square_ref, ring - 1, recv_sems.at[2])
    inverse = as_columns(lax.rsqrt(jnp.sum(square_ref[...], axis=0) + EPS))
    for q in range(chunks):
        here = slice(q * CHUNK, (q + 1) * CHUNK)
        unit = unit_ref[here, :] * scale * inverse[:, q : q + 1]
        unit_ref[here, :] = unit
        normed = (unit * multiplier).reshape(per, cap, width).astype(BF16)
        back_ref[q * per : (q + 1) * per, :, :width] = normed
    exchange(back_ref, done_ref, 3)
    done_ref[me] = back_ref[me]

    wait_blocks(recv_ref, owners - 1, recv_sems.at[1])

    def received(q):
        block = recv_ref[q * per : (q + 1) * per, :, :width].astype(F32)
        return block.reshape(CHUNK, width)

    sums = []
    total = jnp.zeros((1, width), F32)
    for q in range(chunks):
        here = slice(q * CHUNK, (q + 1) * CHUNK)
        product = received(q) * unit_ref[here, :]
        total += jnp.sum(product, axis=0, keepdims=True)
        sums.append(jnp.sum(product * multiplier, axis=1, keepdims=True))
    part_ref[1] = as_rows(sums)
    share(part_ref.at[1], inner_ref, 4, col, ring, along)
    wgp_ref[:, :width] = total
    wgp_ref[:, width:] = jnp.zeros((1, wide - width), F32)
    share(wgp_ref, wg1_ref, 5, inner_id, cores, beside)

    wait_blocks(inner_ref, ring - 1, recv_sems.at[4])
    inner = as_columns(jnp.sum(inner_ref[...], axis=0) * (1.0 / (width * ring)))
    for q in range(chunks):
        here = slice(q * CHUNK, (q + 1) * CHUNK)
        rest = received(q) * multiplier - unit_ref[here, :] * inner[:, q : q + 1]
        g_ref[here, :] = (scale * inverse[:, q : q + 1] * rest).astype(BF16)
    wait_blocks(wg1_ref, cores - 1, recv_sems.at[5])
    wgs_ref[...] = jnp.sum(wg1_ref[...], axis=0)
    share(wgs_ref, wg2_ref, 6, height, heights, above)

    grad_ref[...] = lax.dot_general(
        g_ref[...], hot_ref[...], TN, preferred_element_type=F32
    ).astype(BF16)

    wait_blocks(wg2_ref, heights - 1, recv_sems.at[6])
    wg_ref[...] = jnp.sum(wg2_ref[...], axis=0)[:, :width].reshape(width)
    wait_blocks(done_ref, owners - 1, recv_sems.at[3])
    arrived = done_ref[:, :, :width].astype(F32).reshape(slots, width).astype(BF16)
    normed_ref[...] = lax.dot_general(
        arrived, place_ref[...], TN, preferred_element_type=F32
    ).astype(BF16)

    for n, (ref, number) in enumerate(
        (
            (ask_ref, owners),
            (send_ref, owners),
            (square_ref, ring),
            (back_ref, owners),
            (inner_ref, ring),
            (wg1_ref, cores),
            (wg2_ref, heights),
        )
    ):
        wait_blocks(ref, number - 1, send_sems.at[n])


def body(mesh, token_ids, table, norm_weight, cotangent):
    groups, ring = mesh.shape["dp"], mesh.shape["mp"]
    owners = mesh.shape["section"] * groups
    vrows, width = table.shape
    count = token_ids.shape[0]
    cap = 2 * count // owners
    cores = 8
    heights = owners // cores
    slots = owners * cap
    chunks = slots // CHUNK
    wide = -(-width // 128) * 128
    operands = (token_ids.reshape(1, count), norm_weight, cotangent.T, table.T)
    vmem = pl.BlockSpec(memory_space=pltpu.VMEM)
    hbm = pl.BlockSpec(memory_space=pltpu.HBM)
    normed, weight_grad, table_grad = pl.pallas_call(
        functools.partial(kernel, (groups, ring, cap, cores)),
        out_shape=(
            jax.ShapeDtypeStruct((width, count), BF16),
            jax.ShapeDtypeStruct((width,), F32),
            jax.ShapeDtypeStruct((width, vrows), BF16),
        ),
        in_specs=[hbm, hbm, hbm, hbm],
        out_specs=(vmem, vmem, vmem),
        scratch_shapes=[
            pltpu.VMEM((1, count), jnp.int32),
            pltpu.VMEM((width,), F32),
            pltpu.VMEM((width, vrows), BF16),
            pltpu.VMEM((width, count), BF16),
            pltpu.VMEM((slots, count), BF16),
            pltpu.VMEM((owners, 1, 128), jnp.int32),
            pltpu.VMEM((owners, 1, 128), jnp.int32),
            pltpu.VMEM((owners, cap, wide), BF16),
            pltpu.VMEM((owners, cap, wide), BF16),
            pltpu.VMEM((slots, vrows), BF16),
            pltpu.VMEM((slots, width), F32),
            pltpu.VMEM((2, chunks, 128), F32),
            pltpu.VMEM((ring, chunks, 128), F32),
            pltpu.VMEM((ring, chunks, 128), F32),
            pltpu.VMEM((owners, cap, wide), BF16),
            pltpu.VMEM((owners, cap, wide), BF16),
            pltpu.VMEM((slots, width), BF16),
            pltpu.VMEM((1, wide), F32),
            pltpu.VMEM((cores, 1, wide), F32),
            pltpu.VMEM((1, wide), F32),
            pltpu.VMEM((heights, 1, wide), F32),
            pltpu.SemaphoreType.DMA((4,)),
            pltpu.SemaphoreType.DMA((7,)),
            pltpu.SemaphoreType.DMA((7,)),
        ],
        compiler_params=pltpu.CompilerParams(
            collective_id=0, has_side_effects=True, vmem_limit_bytes=32 * 1024 * 1024
        ),
    )(*(pltpu.with_memory_space_constraint(x, pltpu.HBM) for x in operands))
    return normed.T, weight_grad, table_grad.T


def solution(mesh):
    placed = (P(("section", "dp")), P(("section", "dp"), "mp"), P("mp"), P(("section", "dp"), "mp"))
    return jax.shard_map(
        functools.partial(body, mesh),
        mesh=mesh,
        in_specs=placed,
        out_specs=(P(("section", "dp"), "mp"), P("mp"), P(("section", "dp"), "mp")),
        check_vma=False,
    )
```

time: 67.2 us -> 51.3 us (0.76)
  Pallas kernels: 59.4 us -> 47.5 us
  local copies, waits for them, and re-layouts: 6.11 us -> 2.71 us
    pallas_call x1, Pallas kernels: 59.4 us -> 47.5 us  [body(): pl.pallas_call(functools.partial(kernel, (groups, ring, cap, cores)), out...]
    unnamed x8 -> x3, local copies, waits for them, and re-layouts: 5.42 us -> 2.71 us
    reshape x1 -> x0, local copies, waits for them, and re-layouts: 0.69 us -> none  [body(): norm_weight.reshape(1, width)]
where the time goes in v2:
time: 51.3 us; the launch traced here: 50.9 us
  Pallas kernels  47.5 us (93%)
  local copies, waits for them, and re-layouts  2.71 us (5%)
  between operations  0.64 us (1%)
    pallas_call x1, Pallas kernels, body(): pl.pallas_call(functools.partial(kernel, (groups, ring, cap, cores)), out...  47.5 us
    unnamed x3, local copies, waits for them, and re-layouts  2.71 us

profile of v2, /device:TPU:6, one launch (start us, length us, event | category | flops | bytes accessed | tf_op | source)
XLA Modules:
  0.0 50.9 jit_solution(7064763638886303781)
XLA Ops:
  0.6 47.5 %shard_map.67 = (bf16[576,256]{1,0:T(8,128)(2,1)S(1)}, f32[576]{0:T(1024)S(1)}, bf16[576,2000]{1,0:T(8,128)(2,1)S(1)}) custom-call(s32[1,256]{1,0:T(1,128)} %bitcast.9, f32[576]{0:T(1024)} %weight_hbm.1, bf16[576,256]{1,0:T(8,128)(2,1)} %bitcast.8, bf16[576,2000]{1,0:T(8,128)(2,1)} %bitcast.7), custom_call_target="tpu_custom_call" | custom-call | tf_op jit(solution)/shard_map/pallas_call | solution.py:287
  48.1 0.7 %copy.10 = bf16[256,576]{0,1:T(8,128)(2,1)} copy(bf16[256,576]{0,1:T(8,128)(2,1)S(1)} %bitcast.6) | data formatting | bytes 589824
  48.9 0.6 %copy.11 = f32[576]{0:T(1024)} copy(f32[576]{0:T(1024)S(1)} %get-tuple-element.13) | data formatting | bytes 4608
  49.4 1.4 %copy.12 = bf16[2000,576]{0,1:T(8,128)(2,1)} copy(bf16[2000,576]{0,1:T(8,128)(2,1)S(1)} %bitcast.5) | data formatting | bytes 4608000

commit v3 on v2

--- a/solution.py
+++ b/solution.py
@@ -16,6 +16,7 @@
 TN = (((0,), (0,)), ((), ()))
 
 CHUNK = 128
+STRIP = 64
 
 
 def kernel(
@@ -34,15 +35,19 @@
     place_ref,
     ask_ref,
     asked_ref,
-    send_ref,
-    recv_ref,
+    cot_out_refs,
+    cot_in_refs,
+    row_out_refs,
+    row_in_refs,
     hot_ref,
     unit_ref,
     part_ref,
     square_ref,
     inner_ref,
-    back_ref,
-    done_ref,
+    mult_ref,
+    inv_ref,
+    scaled_ref,
+    square_part_ref,
     g_ref,
     wgp_ref,
     wg1_ref,
@@ -58,7 +63,9 @@
     width, count = cot_ref.shape
     vrows = table_ref.shape[1]
     slots = owners * cap
-    wide = send_ref.shape[2]
+    wide = wgp_ref.shape[1]
+    full = cot_out_refs[0].shape[2]
+    rest = width - full
     scale = math.sqrt(width * ring)
     chunks = slots // CHUNK
     per = CHUNK // cap
@@ -101,7 +108,7 @@
                 (ids_hbm, ids_ref),
                 (cot_hbm, cot_ref),
                 (weight_hbm, weight_ref),
-                (table_hbm, table_ref),
+                (table_hbm, table_ref.at[pl.ds(0, table_hbm.shape[0])]),
             )
         )
     ]
@@ -144,7 +151,11 @@
         @pl.loop(1, owners)
         def _(k):
             p, device = plane(k)
-            send_to(src.at[p], dst.at[me], n, device)
+            for m, (one, other) in enumerate(zip(src, dst)):
+                send_to(one.at[p], other.at[me], n + m, device)
+
+        for one, other in zip(src, dst):
+            other[me] = one[me]
 
     def share(src, dst, n, mine, number, device_of):
         @pl.loop(1, number)
@@ -157,30 +168,69 @@
         part = ref.at[pl.ds(0, number)]
         pltpu.make_async_copy(part, part, sem).wait()
 
+    def put(refs, q, value):
+        block = slice(q * per, (q + 1) * per)
+        refs[0][block] = value[:, :full].reshape(per, cap, full).astype(BF16)
+        last = value[:, full:].reshape(per, cap, rest)
+        last = jnp.concatenate([last[:, : cap // 2], last[:, cap // 2 :]], axis=2)
+        refs[1][block] = last.astype(BF16)
+
+    def get(refs, q):
+        block = slice(q * per, (q + 1) * per)
+        last = refs[1][block].astype(F32)
+        last = jnp.concatenate([last[:, :, :rest], last[:, :, rest:]], axis=1)
+        first = refs[0][block].astype(F32).reshape(CHUNK, full)
+        return jnp.concatenate([first, last.reshape(CHUNK, rest)], axis=1)
+
     pl.semaphore_wait(barrier, owners - 1 + ring - 1)
-    exchange(ask_ref, asked_ref, 0)
-    asked_ref[me] = ask_ref[me]
+    exchange((ask_ref,), (asked_ref,), 0)
+
+    fetches[3].wait()
+    squares = jnp.zeros((1, vrows), F32)
+    for first in range(0, width, STRIP):
+        rows = table_ref[first : first + STRIP, :].astype(F32)
+        squares += jnp.sum(rows * rows, axis=0, keepdims=True)
+    square_part_ref[:, :vrows] = squares
+    square_part_ref[:, vrows:] = jnp.zeros((1, square_part_ref.shape[1] - vrows), F32)
+    share(square_part_ref, square_ref, 3, col, ring, along)
 
     fetches[1].wait()
     for q in range(chunks):
         packed = lax.dot_general(
             place_ref[q * CHUNK : (q + 1) * CHUNK, :], cot_ref[...], NT, preferred_element_type=F32
         )
-        block = slice(q * per, (q + 1) * per)
-        send_ref[block, :, :width] = packed.reshape(per, cap, width).astype(BF16)
-    send_ref[:, :, width:] = jnp.zeros((owners, cap, wide - width), BF16)
-    back_ref[:, :, width:] = jnp.zeros((owners, cap, wide - width), BF16)
-    exchange(send_ref, recv_ref, 1)
-    recv_ref[me] = send_ref[me]
+        put(cot_out_refs, q, packed)
+    exchange(cot_out_refs, cot_in_refs, 1)
 
     fetches[2].wait()
     multiplier = 1.0 + weight_ref[...].reshape(1, width)
-    fetches[3].wait()
+    for first in range(0, width, 128):
+        last = min(first + 128, width)
+        row = jnp.broadcast_to(multiplier[:, first:last], (128, last - first))
+        mult_ref[first:last, :] = row.T
+
+    wait_blocks(square_ref, ring - 1, recv_sems.at[3])
+    inverse = lax.rsqrt(jnp.sum(square_ref[...], axis=0)[:, :vrows] + EPS)
+    for first in range(0, width, STRIP):
+        strip = slice(first, first + STRIP)
+        unit = table_ref[strip, :].astype(F32) * (scale * inverse)
+        scaled_ref[strip, :] = (unit * mult_ref[strip, :1]).astype(BF16)
+    high = inverse.astype(BF16).astype(F32)
+    middle = (inverse - high).astype(BF16).astype(F32)
+    low = inverse - high - middle
+    line = lax.broadcasted_iota(jnp.int32, (16, vrows), 0)
+    pieces = jnp.where(line == 0, high, jnp.where(line == 1, middle, jnp.where(line == 2, low, 0.0)))
+    table_ref[width:, :] = pieces.astype(BF16)
     wait_blocks(asked_ref, owners - 1, recv_sems.at[0])
 
     lane = lax.broadcasted_iota(jnp.int32, (CHUNK, 128), 1)
     own_lane = lane == lax.rem(lax.broadcasted_iota(jnp.int32, (CHUNK, 128), 0), cap)
     entry = lax.broadcasted_iota(jnp.int32, (CHUNK, vrows), 1)
+
+    def per_slot(ref, q, nothing):
+        value = ref[q * per : (q + 1) * per]
+        value = jnp.broadcast_to(value, (per, cap, 128)).reshape(CHUNK, 128)
+        return jnp.sum(jnp.where(own_lane, value, nothing), axis=1, keepdims=True)
 
     def as_rows(columns):
         out = jnp.zeros((CHUNK, 128), F32)
@@ -192,76 +242,68 @@
         filler = jnp.zeros((128 - chunks, 128), F32)
         return jnp.concatenate([rows, filler], axis=0).T
 
-    sums = []
-    for q in range(chunks):
-        here = slice(q * CHUNK, (q + 1) * CHUNK)
-        theirs = asked_ref[q * per : (q + 1) * per]
-        theirs = jnp.broadcast_to(theirs, (per, cap, 128)).reshape(CHUNK, 128)
-        number = jnp.sum(jnp.where(own_lane, theirs, 0), axis=1, keepdims=True)
-        hot_ref[here, :] = jnp.where(number == entry, 1.0, 0.0).astype(BF16)
-        rows = lax.dot_general(hot_ref[here, :], table_ref[...], NT, preferred_element_type=F32)
-        unit_ref[here, :] = rows
-        sums.append(jnp.sum(rows * rows, axis=1, keepdims=True))
-    part_ref[0] = as_rows(sums)
-    share(part_ref.at[0], square_ref, 2, col, ring, along)
-    wait_blocks(square_ref, ring - 1, recv_sems.at[2])
-    inverse = as_columns(lax.rsqrt(jnp.sum(square_ref[...], axis=0) + EPS))
-    for q in range(chunks):
-        here = slice(q * CHUNK, (q + 1) * CHUNK)
-        unit = unit_ref[here, :] * scale * inverse[:, q : q + 1]
-        unit_ref[here, :] = unit
-        normed = (unit * multiplier).reshape(per, cap, width).astype(BF16)
-        back_ref[q * per : (q + 1) * per, :, :width] = normed
-    exchange(back_ref, done_ref, 3)
-    done_ref[me] = back_ref[me]
-
-    wait_blocks(recv_ref, owners - 1, recv_sems.at[1])
-
-    def received(q):
-        block = recv_ref[q * per : (q + 1) * per, :, :width].astype(F32)
-        return block.reshape(CHUNK, width)
-
+    for q in range(chunks):
+        span = slice(q * CHUNK, (q + 1) * CHUNK)
+        number = per_slot(asked_ref, q, 0)
+        hot_ref[span, :] = jnp.where(number == entry, 1.0, 0.0).astype(BF16)
+    normed = lax.dot_general(hot_ref[...], scaled_ref[...], NT, preferred_element_type=F32)
+    for q in range(chunks):
+        put(row_out_refs, q, normed[q * CHUNK : (q + 1) * CHUNK, :])
+    exchange(row_out_refs, row_in_refs, 4)
+
+    found = lax.dot_general(hot_ref[...], table_ref[...], NT, preferred_element_type=F32)
+    inverse = (
+        found[:, width : width + 1] + found[:, width + 1 : width + 2] + found[:, width + 2 : width + 3]
+    )
+    unit_ref[...] = found[:, :width] * (scale * inverse)
+    inv_ref[...] = jnp.broadcast_to(inverse, (slots, 128))
+
+    for n in range(2):
+        wait_blocks(cot_in_refs[n], owners - 1, recv_sems.at[1 + n])
     sums = []
     total = jnp.zeros((1, width), F32)
     for q in range(chunks):
-        here = slice(q * CHUNK, (q + 1) * CHUNK)
-        product = received(q) * unit_ref[here, :]
+        span = slice(q * CHUNK, (q + 1) * CHUNK)
+        product = get(cot_in_refs, q) * unit_ref[span, :]
         total += jnp.sum(product, axis=0, keepdims=True)
         sums.append(jnp.sum(product * multiplier, axis=1, keepdims=True))
-    part_ref[1] = as_rows(sums)
-    share(part_ref.at[1], inner_ref, 4, col, ring, along)
+    part_ref[...] = as_rows(sums)
+    share(part_ref, inner_ref, 6, col, ring, along)
     wgp_ref[:, :width] = total
     wgp_ref[:, width:] = jnp.zeros((1, wide - width), F32)
-    share(wgp_ref, wg1_ref, 5, inner_id, cores, beside)
-
-    wait_blocks(inner_ref, ring - 1, recv_sems.at[4])
+    share(wgp_ref, wg1_ref, 7, inner_id, cores, beside)
+
+    wait_blocks(wg1_ref, cores - 1, recv_sems.at[7])
+    wgs_ref[...] = jnp.sum(wg1_ref[...], axis=0)
+    share(wgs_ref, wg2_ref, 8, height, heights, above)
+    wait_blocks(inner_ref, ring - 1, recv_sems.at[6])
     inner = as_columns(jnp.sum(inner_ref[...], axis=0) * (1.0 / (width * ring)))
     for q in range(chunks):
-        here = slice(q * CHUNK, (q + 1) * CHUNK)
-        rest = received(q) * multiplier - unit_ref[here, :] * inner[:, q : q + 1]
-        g_ref[here, :] = (scale * inverse[:, q : q + 1] * rest).astype(BF16)
-    wait_blocks(wg1_ref, cores - 1, recv_sems.at[5])
-    wgs_ref[...] = jnp.sum(wg1_ref[...], axis=0)
-    share(wgs_ref, wg2_ref, 6, height, heights, above)
+        span = slice(q * CHUNK, (q + 1) * CHUNK)
+        left = get(cot_in_refs, q) * multiplier - unit_ref[span, :] * inner[:, q : q + 1]
+        g_ref[span, :] = (scale * inv_ref[span, :1] * left).astype(BF16)
 
     grad_ref[...] = lax.dot_general(
         g_ref[...], hot_ref[...], TN, preferred_element_type=F32
     ).astype(BF16)
 
-    wait_blocks(wg2_ref, heights - 1, recv_sems.at[6])
+    wait_blocks(wg2_ref, heights - 1, recv_sems.at[8])
     wg_ref[...] = jnp.sum(wg2_ref[...], axis=0)[:, :width].reshape(width)
-    wait_blocks(done_ref, owners - 1, recv_sems.at[3])
-    arrived = done_ref[:, :, :width].astype(F32).reshape(slots, width).astype(BF16)
+    for n in range(2):
+        wait_blocks(row_in_refs[n], owners - 1, recv_sems.at[4 + n])
+    arrived = [get(row_in_refs, q).astype(BF16) for q in range(chunks)]
     normed_ref[...] = lax.dot_general(
-        arrived, place_ref[...], TN, preferred_element_type=F32
+        jnp.concatenate(arrived, axis=0), place_ref[...], TN, preferred_element_type=F32
     ).astype(BF16)
 
     for n, (ref, number) in enumerate(
         (
             (ask_ref, owners),
-            (send_ref, owners),
+            (cot_out_refs[0], owners),
+            (cot_out_refs[1], owners),
             (square_ref, ring),
-            (back_ref, owners),
+            (row_out_refs[0], owners),
+            (row_out_refs[1], owners),
             (inner_ref, ring),
             (wg1_ref, cores),
             (wg2_ref, heights),
@@ -282,6 +324,11 @@
     chunks = slots // CHUNK
     wide = -(-width // 128) * 128
     operands = (token_ids.reshape(1, count), norm_weight, cotangent.T, table.T)
+    full = width // 128 * 128
+    blocks = (
+        pltpu.VMEM((owners, cap, full), BF16),
+        pltpu.VMEM((owners, cap // 2, 2 * (width - full)), BF16),
+    )
     vmem = pl.BlockSpec(memory_space=pltpu.VMEM)
     hbm = pl.BlockSpec(memory_space=pltpu.HBM)
     normed, weight_grad, table_grad = pl.pallas_call(
@@ -296,28 +343,32 @@
         scratch_shapes=[
             pltpu.VMEM((1, count), jnp.int32),
             pltpu.VMEM((width,), F32),
-            pltpu.VMEM((width, vrows), BF16),
+            pltpu.VMEM((width + 16, vrows), BF16),
             pltpu.VMEM((width, count), BF16),
             pltpu.VMEM((slots, count), BF16),
             pltpu.VMEM((owners, 1, 128), jnp.int32),
             pltpu.VMEM((owners, 1, 128), jnp.int32),
-            pltpu.VMEM((owners, cap, wide), BF16),
-            pltpu.VMEM((owners, cap, wide), BF16),
+            blocks,
+            blocks,
+            blocks,
+            blocks,
             pltpu.VMEM((slots, vrows), BF16),
             pltpu.VMEM((slots, width), F32),
-            pltpu.VMEM((2, chunks, 128), F32),
+            pltpu.VMEM((chunks, 128), F32),
+            pltpu.VMEM((ring, 1, -(-vrows // 128) * 128), F32),
             pltpu.VMEM((ring, chunks, 128), F32),
-            pltpu.VMEM((ring, chunks, 128), F32),
-            pltpu.VMEM((owners, cap, wide), BF16),
-            pltpu.VMEM((owners, cap, wide), BF16),
+            pltpu.VMEM((width, 128), F32),
+            pltpu.VMEM((slots, 128), F32),
+            pltpu.VMEM((width, vrows), BF16),
+            pltpu.VMEM((1, -(-vrows // 128) * 128), F32),
             pltpu.VMEM((slots, width), BF16),
             pltpu.VMEM((1, wide), F32),
             pltpu.VMEM((cores, 1, wide), F32),
             pltpu.VMEM((1, wide), F32),
             pltpu.VMEM((heights, 1, wide), F32),
             pltpu.SemaphoreType.DMA((4,)),
-            pltpu.SemaphoreType.DMA((7,)),
-            pltpu.SemaphoreType.DMA((7,)),
+            pltpu.SemaphoreType.DMA((9,)),
+            pltpu.SemaphoreType.DMA((9,)),
         ],
         compiler_params=pltpu.CompilerParams(
             collective_id=0, has_side_effects=True, vmem_limit_bytes=32 * 1024 * 1024

time: 51.3 us -> 48.9 us (0.953)
  Pallas kernels: 47.5 us -> 45.5 us
    pallas_call x1, Pallas kernels: 47.5 us -> 45.5 us  [body(): pl.pallas_call(functools.partial(kernel, (groups, ring, cap, cores)), out...]
where the time goes in v3:
time: 48.9 us; the launch traced here: 48.8 us
  Pallas kernels  45.5 us (93%)
  local copies, waits for them, and re-layouts  2.71 us (6%)
  between operations  0.64 us (1%)
    pallas_call x1, Pallas kernels, body(): pl.pallas_call(functools.partial(kernel, (groups, ring, cap, cores)), out...  45.5 us
    unnamed x3, local copies, waits for them, and re-layouts  2.71 us

profile of v3, /device:TPU:6, one launch (start us, length us, event | category | flops | bytes accessed | tf_op | source)
XLA Modules:
  0.0 48.8 jit_solution(3066757800845840373)
XLA Ops:
  0.6 45.5 %shard_map.67 = (bf16[576,256]{1,0:T(8,128)(2,1)S(1)}, f32[576]{0:T(1024)S(1)}, bf16[576,2000]{1,0:T(8,128)(2,1)S(1)}) custom-call(s32[1,256]{1,0:T(1,128)} %bitcast.9, f32[576]{0:T(1024)} %weight_hbm.1, bf16[576,256]{1,0:T(8,128)(2,1)} %bitcast.8, bf16[576,2000]{1,0:T(8,128)(2,1)} %bitcast.7), custom_call_target="tpu_custom_call" | custom-call | tf_op jit(solution)/shard_map/pallas_call | solution.py:334
  46.1 0.7 %copy.10 = bf16[256,576]{0,1:T(8,128)(2,1)} copy(bf16[256,576]{0,1:T(8,128)(2,1)S(1)} %bitcast.6) | data formatting | bytes 589824
  46.8 0.6 %copy.11 = f32[576]{0:T(1024)} copy(f32[576]{0:T(1024)S(1)} %get-tuple-element.13) | data formatting | bytes 4608
  47.4 1.4 %copy.12 = bf16[2000,576]{0,1:T(8,128)(2,1)} copy(bf16[2000,576]{0,1:T(8,128)(2,1)S(1)} %bitcast.5) | data formatting | bytes 4608000

commit v4 on v3

--- a/solution.py
+++ b/solution.py
@@ -19,26 +19,66 @@
 STRIP = 64
 
 
+def get(refs, q):
+    cap, full = refs[0].shape[1:]
+    rest = refs[1].shape[2] // 2
+    block = slice(q * CHUNK // cap, (q + 1) * CHUNK // cap)
+    last = refs[1][block].astype(F32)
+    last = jnp.concatenate([last[:, :, :rest], last[:, :, rest:]], axis=1)
+    first = refs[0][block].astype(F32).reshape(CHUNK, full)
+    return jnp.concatenate([first, last.reshape(CHUNK, rest)], axis=1)
+
+
+def finish(
+    first_ref,
+    last_ref,
+    place_ref,
+    total_ref,
+    grad_ref,
+    normed_hbm,
+    wg_hbm,
+    grad_hbm,
+    normed_ref,
+    wg_ref,
+    sems,
+):
+    grad_copy = pltpu.make_async_copy(grad_ref, grad_hbm, sems.at[0])
+    grad_copy.start()
+    wg_ref[...] = total_ref[...].reshape(total_ref.shape[1])[: wg_ref.shape[0]]
+    wg_copy = pltpu.make_async_copy(wg_ref, wg_hbm, sems.at[1])
+    wg_copy.start()
+    refs = (first_ref, last_ref)
+    arrived = [get(refs, q).astype(BF16) for q in range(place_ref.shape[0] // CHUNK)]
+    normed_ref[...] = lax.dot_general(
+        jnp.concatenate(arrived, axis=0), place_ref[...], TN, preferred_element_type=F32
+    ).astype(BF16)
+    normed_copy = pltpu.make_async_copy(normed_ref, normed_hbm, sems.at[2])
+    normed_copy.start()
+    grad_copy.wait()
+    wg_copy.wait()
+    normed_copy.wait()
+
+
 def kernel(
     dims,
     ids_hbm,
     weight_hbm,
     cot_hbm,
     table_hbm,
-    normed_ref,
+    row_first_ref,
+    row_last_ref,
+    place_ref,
     wg_ref,
     grad_ref,
     ids_ref,
     weight_ref,
     table_ref,
     cot_ref,
-    place_ref,
     ask_ref,
     asked_ref,
     cot_out_refs,
     cot_in_refs,
     row_out_refs,
-    row_in_refs,
     hot_ref,
     unit_ref,
     part_ref,
@@ -91,9 +131,10 @@
         h = lax.rem(height + step, heights)
         return (lax.div(h, groups) * cores + inner_id, lax.rem(h, groups), col)
 
+    row_in_refs = (row_first_ref, row_last_ref)
     barrier = pltpu.get_barrier_semaphore()
 
-    @pl.loop(1, owners)
+    @pl.loop(1, owners, unroll=7)
     def _(k):
         pl.semaphore_signal(barrier, inc=1, device_id=plane(k)[1], device_id_type=MESH)
 
@@ -148,7 +189,7 @@
         ).start()
 
     def exchange(src, dst, n):
-        @pl.loop(1, owners)
+        @pl.loop(1, owners, unroll=7)
         def _(k):
             p, device = plane(k)
             for m, (one, other) in enumerate(zip(src, dst)):
@@ -175,16 +216,12 @@
         last = jnp.concatenate([last[:, : cap // 2], last[:, cap // 2 :]], axis=2)
         refs[1][block] = last.astype(BF16)
 
-    def get(refs, q):
-        block = slice(q * per, (q + 1) * per)
-        last = refs[1][block].astype(F32)
-        last = jnp.concatenate([last[:, :, :rest], last[:, :, rest:]], axis=1)
-        first = refs[0][block].astype(F32).reshape(CHUNK, full)
-        return jnp.concatenate([first, last.reshape(CHUNK, rest)], axis=1)
-
-    pl.semaphore_wait(barrier, owners - 1 + ring - 1)
-    exchange((ask_ref,), (asked_ref,), 0)
-
+    fetches[1].wait()
+    for q in range(chunks):
+        packed = lax.dot_general(
+            place_ref[q * CHUNK : (q + 1) * CHUNK, :], cot_ref[...], NT, preferred_element_type=F32
+        )
+        put(cot_out_refs, q, packed)
     fetches[3].wait()
     squares = jnp.zeros((1, vrows), F32)
     for first in range(0, width, STRIP):
@@ -192,14 +229,11 @@
         squares += jnp.sum(rows * rows, axis=0, keepdims=True)
     square_part_ref[:, :vrows] = squares
     square_part_ref[:, vrows:] = jnp.zeros((1, square_part_ref.shape[1] - vrows), F32)
+    pl.semaphore_wait(barrier, owners - 1 + ring - 1)
+    exchange((ask_ref,), (asked_ref,), 0)
+
     share(square_part_ref, square_ref, 3, col, ring, along)
 
-    fetches[1].wait()
-    for q in range(chunks):
-        packed = lax.dot_general(
-            place_ref[q * CHUNK : (q + 1) * CHUNK, :], cot_ref[...], NT, preferred_element_type=F32
-        )
-        put(cot_out_refs, q, packed)
     exchange(cot_out_refs, cot_in_refs, 1)
 
     fetches[2].wait()
@@ -288,14 +322,9 @@
     ).astype(BF16)
 
     wait_blocks(wg2_ref, heights - 1, recv_sems.at[8])
-    wg_ref[...] = jnp.sum(wg2_ref[...], axis=0)[:, :width].reshape(width)
+    wg_ref[...] = jnp.sum(wg2_ref[...], axis=0)
     for n in range(2):
         wait_blocks(row_in_refs[n], owners - 1, recv_sems.at[4 + n])
-    arrived = [get(row_in_refs, q).astype(BF16) for q in range(chunks)]
-    normed_ref[...] = lax.dot_general(
-        jnp.concatenate(arrived, axis=0), place_ref[...], TN, preferred_element_type=F32
-    ).astype(BF16)
-
     for n, (ref, number) in enumerate(
         (
             (ask_ref, owners),
@@ -331,24 +360,24 @@
     )
     vmem = pl.BlockSpec(memory_space=pltpu.VMEM)
     hbm = pl.BlockSpec(memory_space=pltpu.HBM)
-    normed, weight_grad, table_grad = pl.pallas_call(
+    block_shapes = tuple(jax.ShapeDtypeStruct(block.shape, BF16) for block in blocks)
+    parts = pl.pallas_call(
         functools.partial(kernel, (groups, ring, cap, cores)),
         out_shape=(
-            jax.ShapeDtypeStruct((width, count), BF16),
-            jax.ShapeDtypeStruct((width,), F32),
+            *block_shapes,
+            jax.ShapeDtypeStruct((slots, count), BF16),
+            jax.ShapeDtypeStruct((1, wide), F32),
             jax.ShapeDtypeStruct((width, vrows), BF16),
         ),
-        in_specs=[hbm, hbm, hbm, hbm],
-        out_specs=(vmem, vmem, vmem),
+        in_specs=[hbm] * 4,
+        out_specs=(vmem,) * 5,
         scratch_shapes=[
             pltpu.VMEM((1, count), jnp.int32),
             pltpu.VMEM((width,), F32),
             pltpu.VMEM((width + 16, vrows), BF16),
             pltpu.VMEM((width, count), BF16),
-            pltpu.VMEM((slots, count), BF16),
             pltpu.VMEM((owners, 1, 128), jnp.int32),
             pltpu.VMEM((owners, 1, 128), jnp.int32),
-            blocks,
             blocks,
             blocks,
             blocks,
@@ -374,6 +403,22 @@
             collective_id=0, has_side_effects=True, vmem_limit_bytes=32 * 1024 * 1024
         ),
     )(*(pltpu.with_memory_space_constraint(x, pltpu.HBM) for x in operands))
+    normed, weight_grad, table_grad = pl.pallas_call(
+        finish,
+        out_shape=(
+            jax.ShapeDtypeStruct((width, count), BF16),
+            jax.ShapeDtypeStruct((width,), F32),
+            jax.ShapeDtypeStruct((width, vrows), BF16),
+        ),
+        in_specs=[vmem] * 5,
+        out_specs=(hbm,) * 3,
+        scratch_shapes=[
+            pltpu.VMEM((width, count), BF16),
+            pltpu.VMEM((width,), F32),
+            pltpu.SemaphoreType.DMA((3,)),
+        ],
+        compiler_params=pltpu.CompilerParams(vmem_limit_bytes=32 * 1024 * 1024),
+    )(*parts)
     return normed.T, weight_grad, table_grad.T
 
 

time: 48.9 us -> 46.2 us (0.945)
  local copies, waits for them, and re-layouts: 2.71 us -> 0 us
    unnamed x3 -> x0, local copies, waits for them, and re-layouts: 2.71 us -> none
    pallas_call x1, Pallas kernels: 45.5 us -> 43.9 us  [body(): pl.pallas_call(functools.partial(kernel, (groups, ring, cap, cores)), out...]
    pallas_call x0 -> x1, Pallas kernels: none -> 1.53 us  [body(): pl.pallas_call(finish, out_shape=(jax.ShapeDtypeStruct((width, count), BF...]
where the time goes in v4:
time: 46.2 us; the launch traced here: 46.1 us
  Pallas kernels  45.4 us (98%)
  between operations  0.64 us (1%)
    pallas_call x1, Pallas kernels, body(): pl.pallas_call(functools.partial(kernel, (groups, ring, cap, cores)), out...  43.9 us
    pallas_call x1, Pallas kernels, body(): pl.pallas_call(finish, out_shape=(jax.ShapeDtypeStruct((width, count), BF...  1.53 us

profile of v4, /device:TPU:6, one launch (start us, length us, event | category | flops | bytes accessed | tf_op | source)
XLA Modules:
  0.0 46.1 jit_solution(1190590520847140774)
XLA Ops:
  0.6 43.9 %shard_map.67 = (bf16[64,8,512]{2,1,0:T(8,128)(2,1)S(1)}, bf16[64,4,128]{2,1,0:T(4,128)(2,1)S(1)}, bf16[512,256]{1,0:T(8,128)(2,1)S(1)}, f32[1,640]{1,0:T(1,128)S(1)}, bf16[576,2000]{1,0:T(8,128)(2,1)S(1)}) custom-call(s32[1,256]{1,0:T(1,128)} %bitcast.7, f32[576]{0:T(1024)} %weight_hbm.1, bf16[576,256]{1,0:T(8,128)(2,1)} %bitcast.6, bf16[576,2000]{1,0:T(8,128)(2,1)} %bitcast.5), custom_call_target="tpu_custom_call" | custom-call | tf_op jit(solution)/shard_map/pallas_call | solution.py:364
  44.5 1.5 %shard_map.68 = (bf16[576,256]{1,0:T(8,128)(2,1)}, f32[576]{0:T(1024)}, bf16[576,2000]{1,0:T(8,128)(2,1)}) custom-call(bf16[64,8,512]{2,1,0:T(8,128)(2,1)S(1)} %get-tuple-element.11.first_ref, bf16[64,4,128]{2,1,0:T(4,128)(2,1)S(1)} %get-tuple-element.12.last_ref, bf16[512,256]{1,0:T(8,128)(2,1)S(1)} %get-tuple-element.13.place_ref, ...), custom_call_target="tpu_custom_call" | custom-call | tf_op jit(solution)/shard_map/pallas_call | solution.py:406

commit v5 on v4

--- a/solution.py
+++ b/solution.py
@@ -16,6 +16,7 @@
 TN = (((0,), (0,)), ((), ()))
 
 CHUNK = 128
+BEHIND = 43
 STRIP = 64
 
 
@@ -83,7 +84,11 @@
     unit_ref,
     part_ref,
     square_ref,
+    square_sum_ref,
+    square_other_ref,
     inner_ref,
+    inner_sum_ref,
+    inner_other_ref,
     mult_ref,
     inv_ref,
     scaled_ref,
@@ -121,8 +126,16 @@
         p = lax.rem(me + step, owners)
         return p, (lax.div(p, groups), lax.rem(p, groups), col)
 
+    half = ring // 2
+    place_in_half = lax.rem(col, half)
+    downward = ((ring - 1, (0, 1)), (half, (half - 1, half - 2)))
+    upward = (half - 1, half)
+
+    def at(c):
+        return (sec, grp, c)
+
     def along(step):
-        return (sec, grp, lax.rem(col + step, ring))
+        return at(col - place_in_half + lax.rem(place_in_half + step, half))
 
     def beside(step):
         return (sec - inner_id + lax.rem(inner_id + step, cores), grp, col)
@@ -138,9 +151,19 @@
     def _(k):
         pl.semaphore_signal(barrier, inc=1, device_id=plane(k)[1], device_id_type=MESH)
 
-    @pl.loop(1, ring)
+    def greet(device):
+        pl.semaphore_signal(barrier, inc=1, device_id=device, device_id_type=MESH)
+
+    @pl.loop(1, half)
     def _(k):
-        pl.semaphore_signal(barrier, inc=1, device_id=along(k), device_id_type=MESH)
+        greet(along(k))
+
+    for sender, receivers in (*downward, (upward[0], (upward[1],))):
+        for receiver in receivers:
+
+            @pl.when(col == receiver)
+            def _():
+                greet(at(sender))
 
     fetches = [
         pltpu.make_async_copy(src, dst, local_sems.at[n])
@@ -178,25 +201,26 @@
     place = jnp.where(rank[:, None, :] == slot_of, 1.0, 0.0).reshape(slots, count)
     place_ref[...] = place.astype(BF16)
 
-    def send_to(src, dst, n, device):
+    def send_to(src, dst, n, device, sent=None):
         pltpu.make_async_remote_copy(
             src_ref=src,
             dst_ref=dst,
-            send_sem=send_sems.at[n],
+            send_sem=send_sems.at[n if sent is None else sent],
             recv_sem=recv_sems.at[n],
             device_id=device,
             device_id_type=MESH,
         ).start()
 
-    def exchange(src, dst, n):
-        @pl.loop(1, owners, unroll=7)
+    def exchange(src, dst, n, first=1, last=owners):
+        @pl.loop(first, last, unroll=7)
         def _(k):
             p, device = plane(k)
             for m, (one, other) in enumerate(zip(src, dst)):
                 send_to(one.at[p], other.at[me], n + m, device)
 
-        for one, other in zip(src, dst):
-            other[me] = one[me]
+        if first == 1:
+            for one, other in zip(src, dst):
+                other[me] = one[me]
 
     def share(src, dst, n, mine, number, device_of):
         @pl.loop(1, number)
@@ -208,6 +232,42 @@
     def wait_blocks(ref, number, sem):
         part = ref.at[pl.ds(0, number)]
         pltpu.make_async_copy(part, part, sem).wait()
+
+    def start_sum(src, gathered, n):
+        share(src, gathered, n, place_in_half, half, along)
+
+    def cross(gathered, summed, other, n, meanwhile=None):
+        wait_blocks(gathered, half - 1, recv_sems.at[n])
+        summed[0] = jnp.sum(gathered[...], axis=0)
+        for sender, receivers in (*downward, (upward[0], (upward[1],))):
+
+            @pl.when(col == sender)
+            def _():
+                for receiver in receivers:
+                    send_to(summed.at[0], other.at[0], n + 1, at(receiver))
+
+        if meanwhile is not None:
+            meanwhile()
+        wait_blocks(other, 1, recv_sems.at[n + 1])
+
+        @pl.when(col == upward[1])
+        def _():
+            for receiver in range(half + 1, ring):
+                send_to(other.at[0], other.at[0], n + 1, at(receiver), n + 2)
+
+        return summed[0] + other[0]
+
+    def end_sum(gathered, n):
+        wait_blocks(gathered, half - 1, send_sems.at[n])
+        for sender, receivers in (*downward, (upward[0], (upward[1],))):
+
+            @pl.when(col == sender)
+            def _():
+                wait_blocks(gathered, len(receivers), send_sems.at[n + 1])
+
+        @pl.when(col == upward[1])
+        def _():
+            wait_blocks(gathered, half - 1, send_sems.at[n + 2])
 
     def put(refs, q, value):
         block = slice(q * per, (q + 1) * per)
@@ -229,10 +289,20 @@
         squares += jnp.sum(rows * rows, axis=0, keepdims=True)
     square_part_ref[:, :vrows] = squares
     square_part_ref[:, vrows:] = jnp.zeros((1, square_part_ref.shape[1] - vrows), F32)
-    pl.semaphore_wait(barrier, owners - 1 + ring - 1)
+    crossing = (*downward, (upward[0], (upward[1],)))
+    for sender, receivers in crossing:
+
+        @pl.when(col == sender)
+        def _():
+            pl.semaphore_wait(barrier, owners - 1 + half - 1 + len(receivers))
+
+    @pl.when((col != crossing[0][0]) & (col != crossing[1][0]) & (col != crossing[2][0]))
+    def _():
+        pl.semaphore_wait(barrier, owners - 1 + half - 1)
+
     exchange((ask_ref,), (asked_ref,), 0)
 
-    share(square_part_ref, square_ref, 3, col, ring, along)
+    start_sum(square_part_ref, square_ref, 7)
 
     exchange(cot_out_refs, cot_in_refs, 1)
 
@@ -243,8 +313,8 @@
         row = jnp.broadcast_to(multiplier[:, first:last], (128, last - first))
         mult_ref[first:last, :] = row.T
 
-    wait_blocks(square_ref, ring - 1, recv_sems.at[3])
-    inverse = lax.rsqrt(jnp.sum(square_ref[...], axis=0)[:, :vrows] + EPS)
+    squares = cross(square_ref, square_sum_ref, square_other_ref, 7)
+    inverse = lax.rsqrt(squares[:, :vrows] + EPS)
     for first in range(0, width, STRIP):
         strip = slice(first, first + STRIP)
         unit = table_ref[strip, :].astype(F32) * (scale * inverse)
@@ -283,7 +353,7 @@
     normed = lax.dot_general(hot_ref[...], scaled_ref[...], NT, preferred_element_type=F32)
     for q in range(chunks):
         put(row_out_refs, q, normed[q * CHUNK : (q + 1) * CHUNK, :])
-    exchange(row_out_refs, row_in_refs, 4)
+    exchange(row_out_refs, row_in_refs, 3, 1, BEHIND)
 
     found = lax.dot_general(hot_ref[...], table_ref[...], NT, preferred_element_type=F32)
     inverse = (
@@ -302,16 +372,19 @@
         total += jnp.sum(product, axis=0, keepdims=True)
         sums.append(jnp.sum(product * multiplier, axis=1, keepdims=True))
     part_ref[...] = as_rows(sums)
-    share(part_ref, inner_ref, 6, col, ring, along)
+    start_sum(part_ref, inner_ref, 10)
     wgp_ref[:, :width] = total
     wgp_ref[:, width:] = jnp.zeros((1, wide - width), F32)
-    share(wgp_ref, wg1_ref, 7, inner_id, cores, beside)
-
-    wait_blocks(wg1_ref, cores - 1, recv_sems.at[7])
-    wgs_ref[...] = jnp.sum(wg1_ref[...], axis=0)
-    share(wgs_ref, wg2_ref, 8, height, heights, above)
-    wait_blocks(inner_ref, ring - 1, recv_sems.at[6])
-    inner = as_columns(jnp.sum(inner_ref[...], axis=0) * (1.0 / (width * ring)))
+    share(wgp_ref, wg1_ref, 5, inner_id, cores, beside)
+    exchange(row_out_refs, row_in_refs, 3, BEHIND, owners)
+
+    def second_step():
+        wait_blocks(wg1_ref, cores - 1, recv_sems.at[5])
+        wgs_ref[...] = jnp.sum(wg1_ref[...], axis=0)
+        share(wgs_ref, wg2_ref, 6, height, heights, above)
+
+    inner = cross(inner_ref, inner_sum_ref, inner_other_ref, 10, second_step)
+    inner = as_columns(inner * (1.0 / (width * ring)))
     for q in range(chunks):
         span = slice(q * CHUNK, (q + 1) * CHUNK)
         left = get(cot_in_refs, q) * multiplier - unit_ref[span, :] * inner[:, q : q + 1]
@@ -321,24 +394,24 @@
         g_ref[...], hot_ref[...], TN, preferred_element_type=F32
     ).astype(BF16)
 
-    wait_blocks(wg2_ref, heights - 1, recv_sems.at[8])
+    wait_blocks(wg2_ref, heights - 1, recv_sems.at[6])
     wg_ref[...] = jnp.sum(wg2_ref[...], axis=0)
     for n in range(2):
-        wait_blocks(row_in_refs[n], owners - 1, recv_sems.at[4 + n])
+        wait_blocks(row_in_refs[n], owners - 1, recv_sems.at[3 + n])
     for n, (ref, number) in enumerate(
         (
             (ask_ref, owners),
             (cot_out_refs[0], owners),
             (cot_out_refs[1], owners),
-            (square_ref, ring),
             (row_out_refs[0], owners),
             (row_out_refs[1], owners),
-            (inner_ref, ring),
             (wg1_ref, cores),
             (wg2_ref, heights),
         )
     ):
         wait_blocks(ref, number - 1, send_sems.at[n])
+    end_sum(square_ref, 7)
+    end_sum(inner_ref, 10)
 
 
 def body(mesh, token_ids, table, norm_weight, cotangent):
@@ -384,8 +457,12 @@
             pltpu.VMEM((slots, vrows), BF16),
             pltpu.VMEM((slots, width), F32),
             pltpu.VMEM((chunks, 128), F32),
-            pltpu.VMEM((ring, 1, -(-vrows // 128) * 128), F32),
-            pltpu.VMEM((ring, chunks, 128), F32),
+            pltpu.VMEM((ring // 2, 1, -(-vrows // 128) * 128), F32),
+            pltpu.VMEM((1, 1, -(-vrows // 128) * 128), F32),
+            pltpu.VMEM((1, 1, -(-vrows // 128) * 128), F32),
+            pltpu.VMEM((ring // 2, chunks, 128), F32),
+            pltpu.VMEM((1, chunks, 128), F32),
+            pltpu.VMEM((1, chunks, 128), F32),
             pltpu.VMEM((width, 128), F32),
             pltpu.VMEM((slots, 128), F32),
             pltpu.VMEM((width, vrows), BF16),
@@ -396,8 +473,8 @@
             pltpu.VMEM((1, wide), F32),
             pltpu.VMEM((heights, 1, wide), F32),
             pltpu.SemaphoreType.DMA((4,)),
-            pltpu.SemaphoreType.DMA((9,)),
-            pltpu.SemaphoreType.DMA((9,)),
+            pltpu.SemaphoreType.DMA((13,)),
+            pltpu.SemaphoreType.DMA((13,)),
         ],
         compiler_params=pltpu.CompilerParams(
             collective_id=0, has_side_effects=True, vmem_limit_bytes=32 * 1024 * 1024

time: 46.2 us -> 43.7 us (0.946); the launches traced: 46.1 us -> 43 us
  Pallas kernels: 45.4 us -> 42.4 us
    pallas_call x1, Pallas kernels: 43.9 us -> 40.8 us  [body(): pl.pallas_call(functools.partial(kernel, (groups, ring, cap, cores)), out...]
where the time goes in v5:
time: 43.7 us; the launch traced here: 43 us
  Pallas kernels  42.4 us (97%)
  between operations  0.64 us (1%)
    pallas_call x1, Pallas kernels, body(): pl.pallas_call(functools.partial(kernel, (groups, ring, cap, cores)), out...  40.8 us
    pallas_call x1, Pallas kernels, body(): pl.pallas_call(finish, out_shape=(jax.ShapeDtypeStruct((width, count), BF...  1.53 us

profile of v5, /device:TPU:6, one launch (start us, length us, event | category | flops | bytes accessed | tf_op | source)
XLA Modules:
  0.0 43.0 jit_solution(16534222345431838205)
XLA Ops:
  0.6 40.8 %shard_map.67 = (bf16[64,8,512]{2,1,0:T(8,128)(2,1)S(1)}, bf16[64,4,128]{2,1,0:T(4,128)(2,1)S(1)}, bf16[512,256]{1,0:T(8,128)(2,1)S(1)}, f32[1,640]{1,0:T(1,128)S(1)}, bf16[576,2000]{1,0:T(8,128)(2,1)S(1)}) custom-call(s32[1,256]{1,0:T(1,128)} %bitcast.7, f32[576]{0:T(1024)} %weight_hbm.1, bf16[576,256]{1,0:T(8,128)(2,1)} %bitcast.6, bf16[576,2000]{1,0:T(8,128)(2,1)} %bitcast.5), custom_call_target="tpu_custom_call" | custom-call | tf_op jit(solution)/shard_map/pallas_call | solution.py:437
  41.5 1.5 %shard_map.68 = (bf16[576,256]{1,0:T(8,128)(2,1)}, f32[576]{0:T(1024)}, bf16[576,2000]{1,0:T(8,128)(2,1)}) custom-call(bf16[64,8,512]{2,1,0:T(8,128)(2,1)S(1)} %get-tuple-element.11.first_ref, bf16[64,4,128]{2,1,0:T(4,128)(2,1)S(1)} %get-tuple-element.12.last_ref, bf16[512,256]{1,0:T(8,128)(2,1)S(1)} %get-tuple-element.13.place_ref, ...), custom_call_target="tpu_custom_call" | custom-call | tf_op jit(solution)/shard_map/pallas_call | solution.py:483
